TPU v7x, 512 devices: a whole 4x4x16 slice. The times are simulated.
512 devices in a mesh: slab: 128 (over z, x, core), col: 4 (over y).
Axes of the slice: x: 4, y: 4, z: 16, core: 2. Of those that a mesh axis runs over, the one named last changes fastest.
Arguments:
- basis: bfloat16 [3, 64, 256, 32, 128], P(None, None, 'slab', 'col')
- cell_map: int32 [256, 32, 128], P('slab', 'col'), may hold values from 0 to 7
- table: float32 [8, 27], replicated, may hold values from 0 to 1, as said below
Outputs:
- next_block: bfloat16 [64, 256, 32, 128], P(None, 'slab', 'col')
- projections: float32 [2, 192, 64], replicated
- triangles: float32 [2, 64, 64], replicated
Inputs may be any that keep to these rules, and one draw needn't show every extreme that they name: `table`: coefficients lie between 0 and 1; the centre one is the largest.
All inputs are finite; a program needn't handle non-finite values.
Results may differ from a plain program's by a relative error of at most 0.027.
Values may be sent and summed in bfloat16 or wider, within the bound.
A program may use at most 64 MiB of HBM per device.

v0:
```python
import jax
import jax.numpy as jnp
from jax import lax
from jax.sharding import PartitionSpec as P


def extended(block, sides, width):
    for axis, dim in sides:
        count = lax.axis_size(axis)
        forward = [(i, i + 1) for i in range(count - 1)]
        backward = [(target, source) for source, target in forward]
        low = lax.ppermute(
            lax.slice_in_dim(block, block.shape[dim] - width, None, axis=dim), axis, forward
        )
        high = lax.ppermute(lax.slice_in_dim(block, 0, width, axis=dim), axis, backward)
        block = jnp.concatenate([low, block, high], axis=dim)
    return block


def apply_stencil(wide, coef):
    depth = wide.shape[3]
    rows_x = wide.shape[1] - 2
    rows_y = wide.shape[2] - 2
    padded = jnp.pad(wide, ((0, 0), (0, 0), (0, 0), (1, 1)))
    total = jnp.zeros((wide.shape[0], rows_x, rows_y, depth), jnp.float32)
    for dx in range(3):
        for dy in range(3):
            for dz in range(3):
                offset = 9 * dx + 3 * dy + dz
                piece = padded[:, dx : dx + rows_x, dy : dy + rows_y, dz : dz + depth].astype(
                    jnp.float32
                )
                total = total + coef[offset][None] * piece
    return total.astype(jnp.bfloat16)


def with_faces(block, coef):
    wide = extended(block, (("slab", 1), ("col", 2)), 1)
    return apply_stencil(wide, coef)


def lookup(cell_map, table):
    classes = table.shape[0]
    onehot = (cell_map[None] == jnp.arange(classes, dtype=jnp.int32)[:, None, None, None]).astype(
        jnp.float32
    )
    return jnp.einsum("ko,kxyz->oxyz", table, onehot, precision=lax.Precision.HIGHEST)


def gram_of(left, right, scale):
    return (
        lax.dot_general(left, right, (((1,), (1,)), ((), ())), preferred_element_type=jnp.float32)
        * scale
    )


def correct(stack, block, coeffs):
    moved = lax.dot_general(
        coeffs.astype(jnp.bfloat16),
        stack,
        (((0,), (0,)), ((), ())),
        preferred_element_type=jnp.float32,
    )
    return (block.astype(jnp.float32) - moved).astype(jnp.bfloat16)


def inner_part(flat, shape_wide):
    lead, span_x, span_y, depth = shape_wide
    cube = flat.reshape(lead, span_x, span_y, depth)
    return cube.reshape(lead, -1)


def orthonormalize(stack_wide, block_wide, shape_wide, scale):
    stack = inner_part(stack_wide, (stack_wide.shape[0],) + shape_wide[1:])
    block_inner = inner_part(block_wide, shape_wide)
    first = lax.psum(gram_of(stack, block_inner, 1.0), ("slab", "col")) * scale
    one_wide = correct(stack_wide, block_wide, first)
    second = (
        lax.psum(gram_of(stack, inner_part(one_wide, shape_wide), 1.0), ("slab", "col")) * scale
    )
    two_wide = correct(stack_wide, one_wide, second)
    two_inner = inner_part(two_wide, shape_wide)
    square = lax.psum(gram_of(two_inner, two_inner, 1.0), ("slab", "col")) * scale
    lower = jnp.linalg.cholesky(square)
    identity = jnp.eye(lower.shape[0], dtype=lower.dtype)
    inverse = lax.linalg.triangular_solve(lower, identity, left_side=True, lower=True)
    result = jnp.dot(
        inverse.astype(jnp.bfloat16), two_wide, preferred_element_type=jnp.float32
    ).astype(jnp.bfloat16)
    return (result, first + second, lower, None)


def shards(basis, cell_map, table):
    count_x, count_y, depth = cell_map.shape
    columns = basis.shape[1]
    devices_x = lax.axis_size("slab")
    devices_y = lax.axis_size("col")
    scale = 1.0 / (count_x * devices_x * count_y * devices_y * depth)
    coef = lookup(cell_map, table)
    flat = basis.reshape(3 * columns, count_x * count_y * depth)
    shape_inner = (columns, count_x, count_y, depth)
    image_first = with_faces(basis[2], coef)
    block_one, proj_one, lower_one, gram_one = orthonormalize(
        flat, image_first.reshape(columns, -1), shape_inner, scale
    )
    image = with_faces(block_one.reshape(shape_inner), coef)
    stack = jnp.concatenate([flat[columns:], block_one], axis=0)
    block_two, proj_two, lower_two, gram_two = orthonormalize(
        stack, image.reshape(columns, -1), shape_inner, scale
    )
    return (
        block_two.reshape(shape_inner),
        jnp.stack([proj_one, proj_two]),
        jnp.stack([lower_one, lower_two]),
    )


def solution(mesh):
    placed = (P(None, None, "slab", "col", None), P("slab", "col", None), P())
    return jax.shard_map(
        shards,
        mesh=mesh,
        in_specs=placed,
        out_specs=(P(None, "slab", "col", None), P(), P()),
        check_vma=False,
    )
```

profile of v0, /device:TPU:1, one launch (start us, length us, event | category | flops | bytes accessed | tf_op | source)
XLA Modules:
  0.0 697.7 jit_solution(16092930886953120736)
XLA Ops:
  1.7 4.5 collective-permute-start
  6.2 5.6 collective-permute-start.1
  13.2 2.7 collective-permute-start.2
  18.1 4.1 collective-permute-done.3
  22.2 2.8 fusion.11
  25.0 3.4 add_convert_fusion.1
  28.7 111.1 %psum.42 = f32[192,64]{0,1:T(8,128)S(1)} all-reduce(f32[192,64]{0,1:T(8,128)S(1)} %convolution_bitcast_fusion.2), channel_id=1, replica_groups=mesh['slab'=128,'col'=4] {'slab','col'}, use_global_device_ids=true, to_apply=%region_0.1 | all-reduce | flops 12288 | bytes 98304 | tf_op jit(solution)/shard_map/psum | solution.py:76
  140.5 99.1 %psum.43 = f32[192,64]{0,1:T(8,128)S(1)} all-reduce(f32[192,64]{0,1:T(8,128)S(1)} %convolution_bitcast_fusion.1), channel_id=1, replica_groups=mesh['slab'=128,'col'=4] {'slab','col'}, use_global_device_ids=true, to_apply=%region_1.2 | all-reduce | flops 12288 | bytes 98304 | tf_op jit(solution)/shard_map/psum | solution.py:79
  240.1 100.3 %psum.44 = f32[64,64]{0,1:T(8,128)S(1)} all-reduce(f32[64,64]{0,1:T(8,128)S(1)} %fusion.50), channel_id=1, replica_groups=mesh['slab'=128,'col'=4] {'slab','col'}, use_global_device_ids=true, to_apply=%region_2.3 | all-reduce | flops 4096 | bytes 32768 | tf_op jit(solution)/shard_map/psum | solution.py:83
  340.5 5.8 cholesky.44
  347.7 4.9 custom-call.6
  353.1 3.6 collective-permute-start.4
  357.0 1.9 collective-permute-start.5
  359.0 4.3 collective-permute-done.5
  363.5 1.3 collective-permute-start.6
  364.9 1.5 collective-permute-start.7
  366.8 4.0 collective-permute-done.7
  370.8 1.9 select_maximum_fusion
  372.7 3.3 add_convert_fusion
  376.4 105.5 %psum.45 = f32[192,64]{0,1:T(8,128)S(1)} all-reduce(f32[192,64]{0,1:T(8,128)S(1)} %fusion.15), channel_id=1, replica_groups=mesh['slab'=128,'col'=4] {'slab','col'}, use_global_device_ids=true, to_apply=%region_5.0 | all-reduce | flops 12288 | bytes 98304 | tf_op jit(solution)/shard_map/psum | solution.py:76
  482.6 99.5 %psum.46 = f32[192,64]{0,1:T(8,128)S(1)} all-reduce(f32[192,64]{0,1:T(8,128)S(1)} %fusion.44), channel_id=1, replica_groups=mesh['slab'=128,'col'=4] {'slab','col'}, use_global_device_ids=true, to_apply=%region_6.9 | all-reduce | flops 12288 | bytes 98304 | tf_op jit(solution)/shard_map/psum | solution.py:79
  582.6 100.3 %psum.47 = f32[64,64]{0,1:T(8,128)S(1)} all-reduce(f32[64,64]{0,1:T(8,128)S(1)} %fusion.51), channel_id=1, replica_groups=mesh['slab'=128,'col'=4] {'slab','col'}, use_global_device_ids=true, to_apply=%region_7.10 | all-reduce | flops 4096 | bytes 32768 | tf_op jit(solution)/shard_map/psum | solution.py:83
  683.0 5.8 cholesky.55
  690.2 4.9 custom-call.7
  (57 shorter events, 14.3 us)
Async XLA Ops:
  0.6 11.2 %copy-start = (f32[8,27]{1,0:T(8,128)S(1)}, f32[8,27]{1,0:T(8,128)}, u32[]{:S(2)}) copy-start(f32[8,27]{1,0:T(8,128)} %param.8) | copy-start | bytes 2596
  0.6 16.7 %copy-start.1 = (bf16[3,64,2,8,128]{4,3,2,1,0:T(8,128)(2,1)S(1)}, bf16[3,64,2,8,128]{4,3,2,1,0:T(8,128)(2,1)}, u32[]{:S(2)}) copy-start(bf16[3,64,2,8,128]{4,3,2,1,0:T(8,128)(2,1)} %param.6) | copy-start | bytes 2359300
  1.7 11.2 %collective-permute-start = (bf16[64,1,8,128]{3,2,1,0:T(8,128)(2,1)S(1)}, bf16[64,1,8,128]{3,2,1,0:T(8,128)(2,1)S(1)}, u32[]{:S(2)}, u32[]{:S(2)}) collective-permute-start(bf16[64,1,8,128]{3,2,1,0:T(8,128)(2,1)S(1)} %get-tuple-element.38), channel_id=1, source_target_pairs={{0,4},{4,8},{8,12},{12,16},{16,20},{20,24},{24,28},{28,32},{32,36}... | collective-permute-start | bytes 393224 | tf_op jit(solution)/shard_map/ppermute | solution.py:12
  6.2 6.7 collective-permute-start.1
  13.2 4.9 collective-permute-start.2
  15.9 6.3 collective-permute-start.3
  239.8 116.9 %slice-start = ((bf16[3,64,2,8,128]{4,3,2,1,0:T(8,128)(2,1)}), bf16[2,64,2,8,128]{4,3,2,1,0:T(8,128)(2,1)S(1)}, s32[]{:S(2)}) async-start(bf16[3,64,2,8,128]{4,3,2,1,0:T(8,128)(2,1)} %param.6), calls=%async_computation | async-start | bytes 1048576 | tf_op jit(solution)/shard_map/slice | solution.py:107
  353.1 5.8 collective-permute-start.4
  357.0 6.3 collective-permute-start.5
  363.5 3.3 collective-permute-start.6
  364.9 5.9 collective-permute-start.7
where the time goes:
time: 699 us; the launch traced here: 698 us
  blocking collectives  616 us (88%)
  other arithmetic  37 us (5%)
  starting transfers between devices  22.5 us (3%)
  waiting for transfers between devices  13.3 us (2%)
    psum x2, blocking collectives, orthonormalize(): first = lax.psum(gram_of(stack, block_inner, 1.0), ('slab', 'col')) * scale  217 us
    psum x2, blocking collectives, orthonormalize(): lax.psum(gram_of(two_inner, two_inner, 1.0), ('slab', 'col')) * scale  201 us
    psum x2, blocking collectives, orthonormalize(): lax.psum(gram_of(stack, inner_part(one_wide, shape_wide), 1.0), ('slab',...  199 us
  transfers between devices with their start and end apart: 8, of which 5 were waited for; matrix products, arithmetic and copies ran while one was open for 0% of the time, Pallas kernels for 0%

commit v1 on v0

v1 whole, which is shorter than its diff:
```python
import functools

import jax
import jax.numpy as jnp
from jax import lax
from jax.experimental import pallas as pl
from jax.experimental.pallas import tpu as pltpu
from jax.sharding import PartitionSpec as P

MESH = pl.DeviceIdType.MESH
F32 = jnp.float32
BF16 = jnp.bfloat16
HIGHEST = lax.Precision.HIGHEST
C = 64
NT = (((1,), (1,)), ((), ()))
NN = (((1,), (0,)), ((), ()))
B1, B2, B0, IM = (pl.ds(i * C, C) for i in range(4))


def fdot(a, b, dims):
    return lax.dot_general(a, b, dims, precision=HIGHEST, preferred_element_type=F32)


def places():
    s = lax.axis_index("slab")
    y = lax.axis_index("col")
    z, r = lax.div(s, 8), lax.rem(s, 8)
    rs = [r] + [lax.rem(r + d, 8) for d in range(1, 8)]
    ys = [y] + [lax.rem(y + d, 4) for d in range(1, 4)]
    zs = [z] + [lax.rem(z + d, 16) for d in range(1, 16)]
    plane = [(z * 8 + a, b) for i, a in enumerate(rs) for j, b in enumerate(ys) if i or j]
    chunk = [a * 4 + b for i, a in enumerate(rs) for j, b in enumerate(ys) if i or j]
    column = [(a * 8 + r, y) for a in zs[1:]]
    sl = [s, lax.rem(s + 1, 128), lax.rem(s + 127, 128)]
    near = [(sl[i], ys[j]) for i in (0, 1, 2) for j in (0, 1, 3) if i or j]
    return s, y, z, r * 4 + y, plane, chunk, column, near


def halo_copies(xe, rows, sems, near):
    x_src = {0: pl.ds(1, 2), 1: pl.ds(2, 1), 2: pl.ds(1, 1)}
    x_dst = {0: pl.ds(1, 2), 1: pl.ds(0, 1), 2: pl.ds(3, 1)}
    y_src = {0: pl.ds(1, 8), 1: pl.ds(8, 1), 3: pl.ds(1, 1)}
    y_dst = {0: pl.ds(1, 8), 1: pl.ds(0, 1), 3: pl.ds(9, 1)}
    out = []
    k = 0
    for i in (0, 1, 2):
        for j in (0, 1, 3):
            if i or j:
                out.append(
                    pltpu.make_async_remote_copy(
                        xe.at[x_src[i], y_src[j], rows],
                        xe.at[x_dst[i], y_dst[j], rows],
                        sems.at[0],
                        sems.at[1],
                        device_id=near[k],
                        device_id_type=MESH,
                    )
                )
                k += 1
    return out


def wait_bytes(ref, sem):
    pltpu.make_async_copy(ref, ref, sem).wait()


class Sum:
    def __init__(self, size, src, parts, tower, out, sems, place):
        self.n, self.src, self.parts, self.tower, self.out, self.sems = size, src, parts, tower, out, sems
        _, _, self.z, p, self.plane, self.chunk, self.column, _ = place
        self.mine = pl.ds(pl.multiple_of(p * size, size), size)

    def send(self, src, dst, pair, dev):
        pltpu.make_async_remote_copy(
            src, dst, self.sems.at[pair], self.sems.at[pair + 1], device_id=dev, device_id_type=MESH
        ).start()

    def scatter(self):
        for k, dev in enumerate(self.plane):
            at = pl.ds(pl.multiple_of(self.chunk[k] * self.n, self.n), self.n)
            self.send(self.src.at[at], self.parts.at[k], 0, dev)

    def climb(self):
        wait_bytes(self.parts, self.sems.at[1])
        total = self.src[self.mine, :]
        for k in range(31):
            total = total + self.parts[k]
        self.tower[self.z] = total
        for dev in self.column:
            self.send(self.tower.at[self.z], self.tower.at[self.z], 2, dev)

    def spread(self):
        wait_bytes(self.tower.at[pl.ds(0, 15)], self.sems.at[3])
        total = self.tower[0]
        for k in range(1, 16):
            total = total + self.tower[k]
        self.out[self.mine, :] = total
        for dev in self.plane:
            self.send(self.out.at[self.mine], self.out.at[self.mine], 4, dev)

    def collect(self):
        wait_bytes(self.out.at[pl.ds(0, 31 * self.n)], self.sems.at[5])

    def drain(self):
        wait_bytes(self.parts, self.sems.at[0])
        wait_bytes(self.tower.at[pl.ds(0, 15)], self.sems.at[2])
        wait_bytes(self.out.at[pl.ds(0, 31 * self.n)], self.sems.at[4])


def relayout(basis, xe, wide):
    for b, rows in ((2, B2), (0, B0), (1, B1)):
        for x in range(2):
            wide[...] = basis[b, :, x].astype(F32).reshape(C * 8, 128)
            for y in range(8):
                xe[1 + x, 1 + y, rows, :] = wide[pl.ds(y, C, stride=8), :].astype(BF16)


def coefficients(cell_map, table, coef, s, ycol):
    row = lax.broadcasted_iota(jnp.int32, (8, 128), 0)
    lane = lax.broadcasted_iota(jnp.int32, (8, 128), 1)
    one = jnp.ones((8, 128), F32)
    zero = jnp.zeros((8, 128), F32)
    y_low = jnp.where((row == 0) & (ycol == 0), zero, one)
    y_high = jnp.where((row == 7) & (ycol == 3), zero, one)
    for x in range(2):
        cells = cell_map[x]
        is_class = [cells == k for k in range(8)]
        for o in range(27):
            dx, dy, dz = o // 9, o // 3 % 3, o % 3
            c = zero
            for k in range(8):
                c = jnp.where(is_class[k], table[k, o], c)
            if dx == 0 and x == 0:
                c = jnp.where(s == 0, zero, c)
            if dx == 2 and x == 1:
                c = jnp.where(s == 127, zero, c)
            if dy == 0:
                c = c * y_low
            if dy == 2:
                c = c * y_high
            if dz == 0:
                c = pltpu.roll(jnp.where(lane == 0, zero, c), 127, 1)
            if dz == 2:
                c = pltpu.roll(jnp.where(lane == 127, zero, c), 1, 1)
            coef[pl.ds(x * 8 * 32 + o, 8, stride=32), :] = c


def stencil(xe, rows_in, rows_out, coef):
    for x in range(2):

        def body(y, carry):
            table = coef.at[pl.ds(pl.multiple_of((x * 8 + y) * 32, 32), 32)]
            acc = [jnp.zeros((C, 128), F32) for _ in range(3)]
            for dx in range(3):
                for dy in range(3):
                    piece = xe[x + dx, y + dy, rows_in, :].astype(F32)
                    for dz in range(3):
                        o = 9 * dx + 3 * dy + dz
                        acc[dz] = acc[dz] + table[o : o + 1, :] * piece
            total = acc[1] + pltpu.roll(acc[0], 1, 1) + pltpu.roll(acc[2], 127, 1)
            xe[x + 1, y + 1, rows_out, :] = total.astype(BF16)
            return carry

        lax.fori_loop(0, 8, body, 0)


def gram(xe, rows, count):
    def body(k, acc):
        x, y = k // 8, k % 8
        left = xe[x + 1, y + 1, rows, :]
        right = xe[x + 1, y + 1]
        return acc + lax.dot_general(left, right, NT, preferred_element_type=F32)

    return lax.fori_loop(0, 16, body, jnp.zeros((count, 256), F32))


def project(f_full, g):
    col = lax.broadcasted_iota(jnp.int32, (C, 256), 1)
    keep = col < 192
    first = jnp.where(keep, f_full, 0.0)
    first_b = first.astype(BF16).astype(F32)
    second = jnp.where(keep, first - fdot(first_b, g, NN), 0.0)
    second_b = second.astype(BF16).astype(F32)
    rest = jnp.where(keep, second - fdot(second_b, g, NN), 0.0)
    both = first_b + second_b
    pad = jnp.zeros((C, 256), F32)
    lane = lax.broadcasted_iota(jnp.int32, (C, 128), 1)
    row = lax.broadcasted_iota(jnp.int32, (C, 128), 0)
    own = pltpu.roll(f_full[:, 128:256], 64, 1)
    square = (
        own
        - fdot(first, jnp.concatenate([both, pad], axis=0), NT)
        - fdot(both, jnp.concatenate([rest, pad], axis=0), NT)
    )
    system = jnp.where(lane < C, square, jnp.where(lane == row + C, 1.0, 0.0))
    return first + second, both, rest, system


def factor(m):
    row = lax.broadcasted_iota(jnp.int32, (C, 128), 0)
    diag = jnp.ones((C, 128), F32)
    for j in range(C):
        top = m[j : j + 1, :]
        pivot = m[j : j + 1, j : j + 1]
        diag = jnp.where(row == j, pivot, diag)
        if j < C - 1:
            ratio = jnp.where(row > j, m[:, j : j + 1] / pivot, 0.0)
            m = m - ratio * top
    return m * lax.rsqrt(diag)


def split(v):
    high = v.astype(BF16)
    return high, (v - high.astype(F32)).astype(BF16)


def kernel(
    table, basis, cell_map,
    out_block, out_proj, out_tri,
    xe, wide, coef, src1, parts1, tower1, sum1, src2, parts2, tower2, sum2, gm, halo_sems, sum_sems,
):
    place = places()
    s, ycol, z, p, plane, chunk, column, near = place
    barrier = pltpu.get_barrier_semaphore()
    for dev in plane + column + near:
        pl.semaphore_signal(barrier, inc=1, device_id=dev, device_id_type=MESH)

    relayout(basis, xe, wide)
    coefficients(cell_map, table, coef, s, ycol)

    pl.semaphore_wait(barrier, len(plane + column + near))
    for copy in halo_copies(xe, B2, halo_sems.at[0], near):
        copy.start()
    for k, rows in ((1, B0), (2, B1)):
        for copy in halo_copies(xe, rows, halo_sems.at[k], near):
            copy.start()
    moved = xe.at[pl.ds(0, 3), pl.ds(0, 8), B2]
    wait_bytes(moved, halo_sems.at[0, 1])
    stencil(xe, B2, IM, coef)

    one = Sum(16, src1, parts1, tower1, sum1, sum_sems.at[0], place)
    two = Sum(8, src2, parts2, tower2, sum2, sum_sems.at[1], place)
    g = gram(xe, pl.ds(0, 256), 256)
    src1[0:256, :] = g[:, 0:128]
    src1[256:512, :] = g[:, 128:256]
    one.scatter()
    for copy in halo_copies(xe, IM, halo_sems.at[3], near):
        copy.start()
    one.climb()
    one.spread()
    one.collect()

    scale = 1.0 / (256 * 32 * 128)
    g = jnp.concatenate([sum1[0:256, :], sum1[256:512, :]], axis=1) * scale
    gm[...] = g
    proj, both, rest, system = project(g[192:256, :], g)
    out_proj[0] = proj

    col = lax.broadcasted_iota(jnp.int32, (C, 256), 1)
    row = lax.broadcasted_iota(jnp.int32, (C, 256), 0)
    high, low = split(jnp.where(col == row + 192, 1.0, -both))
    for k in range(4):
        wait_bytes(moved, halo_sems.at[k, 0])
        if k:
            wait_bytes(moved, halo_sems.at[k, 1])

    def correct(k, carry):
        x, y = k // 10, k % 10
        v = xe[x, y]
        w = lax.dot_general(high, v, NN, preferred_element_type=F32)
        w = w + lax.dot_general(low, v, NN, preferred_element_type=F32)
        xe[x, y, B0, :] = w.astype(BF16)
        return carry

    lax.fori_loop(0, 40, correct, 0)
    stencil(xe, B0, IM, coef)

    h = gram(xe, pl.ds(128, 128), 128)
    src2[0:128, :] = h[:, 0:128]
    src2[128:256, :] = h[:, 128:256]
    two.scatter()
    two.climb()

    done = factor(system)
    out_tri[0] = done
    inverse = pltpu.roll(done, 64, 1)[:, 0:C].astype(BF16).astype(F32)
    zero = jnp.zeros((C, C), F32)
    q_left = fdot(inverse, rest[:, 0:128], NN)
    q_own = fdot(fdot(inverse, system[:, 0:C], NN), inverse, NT)
    gm[128:192, 0:128] = q_left
    gm[0:128, 128:192] = jnp.transpose(q_left)
    gm[128:192, 128:192] = q_own
    twice = jnp.concatenate(
        [jnp.concatenate([inverse, zero], axis=1), jnp.concatenate([zero, inverse], axis=1)], axis=0
    )

    two.spread()
    two.collect()
    h = jnp.concatenate([sum2[64:128, :], sum2[192:256, :]], axis=1) * scale
    h = fdot(inverse, h, NN)
    f_full = jnp.concatenate([h[:, 0:128], fdot(h[:, 128:256], twice, NT)], axis=1)
    proj, both, rest, system = project(f_full, gm[...])
    out_proj[1] = proj
    lane = lax.broadcasted_iota(jnp.int32, (C, 128), 1)
    mixed = jnp.where(lane < C, -both[:, 128:256], jnp.where(lane == lax.broadcasted_iota(jnp.int32, (C, 128), 0) + C, 1.0, 0.0))
    mixed = fdot(mixed, twice, NN)
    high2, low2 = split(jnp.concatenate([-both[:, 0:128], mixed], axis=1))
    done = factor(system)
    out_tri[1] = done
    inverse2 = pltpu.roll(done, 64, 1)[:, 0:C].astype(BF16)
    for x in range(2):

        def finish(y, carry):
            v = xe[x + 1, y + 1]
            w = lax.dot_general(high2, v, NN, preferred_element_type=F32)
            w = w + lax.dot_general(low2, v, NN, preferred_element_type=F32)
            wide[pl.ds(y, C, stride=8), :] = lax.dot_general(inverse2, w.astype(BF16), NN, preferred_element_type=F32)
            return carry

        lax.fori_loop(0, 8, finish, 0)
        out_block[:, x] = wide[...].reshape(C, 8, 128).astype(BF16)
    one.drain()
    two.drain()


def shards(basis, cell_map, table):
    vmem = pl.BlockSpec(memory_space=pltpu.VMEM)
    block, proj, tri = pl.pallas_call(
        kernel,
        out_shape=(
            jax.ShapeDtypeStruct((C, 2, 8, 128), BF16),
            jax.ShapeDtypeStruct((2, C, 256), F32),
            jax.ShapeDtypeStruct((2, C, 128), F32),
        ),
        in_specs=[pl.BlockSpec(memory_space=pltpu.SMEM), vmem, vmem],
        out_specs=(vmem, vmem, vmem),
        scratch_shapes=[
            pltpu.VMEM((4, 10, 256, 128), BF16),
            pltpu.VMEM((C * 8, 128), F32),
            pltpu.VMEM((16 * 32, 128), F32),
            pltpu.VMEM((512, 128), F32),
            pltpu.VMEM((31, 16, 128), F32),
            pltpu.VMEM((16, 16, 128), F32),
            pltpu.VMEM((512, 128), F32),
            pltpu.VMEM((256, 128), F32),
            pltpu.VMEM((31, 8, 128), F32),
            pltpu.VMEM((16, 8, 128), F32),
            pltpu.VMEM((256, 128), F32),
            pltpu.VMEM((256, 256), F32),
            pltpu.SemaphoreType.DMA((4, 2)),
            pltpu.SemaphoreType.DMA((2, 6)),
        ],
        compiler_params=pltpu.CompilerParams(
            collective_id=0, has_side_effects=True, vmem_limit_bytes=40 * 1024 * 1024
        ),
    )(table, basis, cell_map)
    proj = jnp.swapaxes(proj, 1, 2)
    first = jnp.concatenate([proj[0, 128:192], proj[0, 0:128]], axis=0)
    lower = jnp.tril(jnp.swapaxes(tri[:, :, 0:C], 1, 2))
    return block, jnp.stack([first, proj[1, 0:192]]), lower


def solution(mesh):
    placed = (P(None, None, "slab", "col", None), P("slab", "col", None), P())
    return jax.shard_map(
        shards,
        mesh=mesh,
        in_specs=placed,
        out_specs=(P(None, "slab", "col", None), P(), P()),
        check_vma=False,
    )
```

time: 699 us -> 105 us (0.15)
  blocking collectives: 616 us -> 0 us
  Pallas kernels: 0 us -> 99.7 us
  other arithmetic: 37 us -> 0.76 us
  starting transfers between devices: 22.5 us -> 0 us
  waiting for transfers between devices: 13.3 us -> 0 us
    psum x6 -> x0, blocking collectives: 616 us -> none  [the longest x2 217 us: orthonormalize(): first = lax.psum(gram_of(stack, block_inner, 1.0), ('slab', 'col')) * scale]
    pallas_call x0 -> x1, Pallas kernels: none -> 99.7 us  [shards(): pl.pallas_call(kernel, out_shape=(jax.ShapeDtypeStruct((C, 2, 8, 128), BF...]
    another operation x14 -> x2, other arithmetic: 25.5 us -> 0.74 us  [shards(): return (block, jnp.stack([first, proj[1, 0:192]]), lower)]
    ppermute x8 -> x0, starting transfers between devices: 22.5 us -> none  [the longest x4 12.2 us: extended(): lax.ppermute(lax.slice_in_dim(block, block.shape[dim] - width, None, axis...]
    ppermute x8 -> x0, waiting for transfers between devices: 13.3 us -> none  [the longest x4 12.4 us: extended(): lax.ppermute(lax.slice_in_dim(block, 0, width, axis=dim), axis, backward)]
  transfers between devices with their start and end apart: 8 -> 0, of which waited for: 5 -> 0; matrix products, arithmetic and copies ran while one was open for 0% -> 0% of each run, Pallas kernels for 0% -> 0%
where the time goes in v1:
time: 105 us
  Pallas kernels  99.7 us (95%)
  local copies, waits for them, and re-layouts  3.94 us (4%)
    pallas_call x1, Pallas kernels, shards(): pl.pallas_call(kernel, out_shape=(jax.ShapeDtypeStruct((C, 2, 8, 128), BF...  99.7 us
    unnamed x8, local copies, waits for them, and re-layouts  3.92 us

profile of v1, /device:TPU:1, one launch (start us, length us, event | category | flops | bytes accessed | tf_op | source)
XLA Modules:
  0.0 105.1 jit_solution(5092251505591224308)
XLA Ops:
  0.6 0.0 copy-start
  0.6 1.1 %copy-done = bf16[3,64,2,8,128]{4,3,2,1,0:T(8,128)(2,1)S(1)} copy-done((bf16[3,64,2,8,128]{4,3,2,1,0:T(8,128)(2,1)S(1)}, bf16[3,64,2,8,128]{4,3,2,1,0:T(8,128)(2,1)}, u32[]{:S(2)}) %copy-start) | copy-done | bytes 786456
  1.8 0.0 copy-start.1
  1.8 0.7 copy-done.1
  2.5 0.0 copy-start.2
  2.5 0.7 copy-done.2
  3.1 99.7 %shard_map.58 = (bf16[64,2,8,128]{3,2,1,0:T(8,128)(2,1)S(1)}, f32[2,64,256]{2,1,0:T(8,128)S(1)}, f32[2,64,128]{2,1,0:T(8,128)S(1)}) custom-call(f32[8,27]{1,0:T(8,128)S(1)} %copy-done.2, bf16[3,64,2,8,128]{4,3,2,1,0:T(8,128)(2,1)S(1)} %copy-done, s32[2,8,128]{2,1,0:T(8,128)S(1)} %copy-done.1), custom_call_target="tpu_custom_call" | custom-call | tf_op jit(solution)/shard_map/pallas_call | solution.py:328
  102.9 0.1 maximum_bitcast_fusion
  103.0 0.7 pad_maximum_fusion
  103.7 0.7 copy.6
  104.4 0.7 copy.8
  (5 shorter events, 0.0 us)
Async XLA Ops:
  0.6 1.1 %copy-start = (bf16[3,64,2,8,128]{4,3,2,1,0:T(8,128)(2,1)S(1)}, bf16[3,64,2,8,128]{4,3,2,1,0:T(8,128)(2,1)}, u32[]{:S(2)}) copy-start(bf16[3,64,2,8,128]{4,3,2,1,0:T(8,128)(2,1)} %basis.1) | copy-start | bytes 2359300
  1.8 0.7 copy-start.1
  2.5 0.7 copy-start.2

commit v2 on v1

--- a/solution.py
+++ b/solution.py
@@ -65,10 +65,9 @@
 
 
 class Sum:
-    def __init__(self, size, src, parts, tower, out, sems, place):
-        self.n, self.src, self.parts, self.tower, self.out, self.sems = size, src, parts, tower, out, sems
-        _, _, self.z, p, self.plane, self.chunk, self.column, _ = place
-        self.mine = pl.ds(pl.multiple_of(p * size, size), size)
+    def __init__(self, src, parts, tower, out, sems, place):
+        self.src, self.parts, self.tower, self.out, self.sems = src, parts, tower, out, sems
+        _, _, self.z, self.mine, self.plane, self.chunk, self.column, _ = place
 
     def send(self, src, dst, pair, dev):
         pltpu.make_async_remote_copy(
@@ -77,12 +76,11 @@
 
     def scatter(self):
         for k, dev in enumerate(self.plane):
-            at = pl.ds(pl.multiple_of(self.chunk[k] * self.n, self.n), self.n)
-            self.send(self.src.at[at], self.parts.at[k], 0, dev)
+            self.send(self.src.at[self.chunk[k]], self.parts.at[k], 0, dev)
 
     def climb(self):
         wait_bytes(self.parts, self.sems.at[1])
-        total = self.src[self.mine, :]
+        total = self.src[self.mine]
         for k in range(31):
             total = total + self.parts[k]
         self.tower[self.z] = total
@@ -94,17 +92,17 @@
         total = self.tower[0]
         for k in range(1, 16):
             total = total + self.tower[k]
-        self.out[self.mine, :] = total
+        self.out[self.mine] = total
         for dev in self.plane:
             self.send(self.out.at[self.mine], self.out.at[self.mine], 4, dev)
 
     def collect(self):
-        wait_bytes(self.out.at[pl.ds(0, 31 * self.n)], self.sems.at[5])
+        wait_bytes(self.out.at[pl.ds(0, 31)], self.sems.at[5])
 
     def drain(self):
         wait_bytes(self.parts, self.sems.at[0])
         wait_bytes(self.tower.at[pl.ds(0, 15)], self.sems.at[2])
-        wait_bytes(self.out.at[pl.ds(0, 31 * self.n)], self.sems.at[4])
+        wait_bytes(self.out.at[pl.ds(0, 31)], self.sems.at[4])
 
 
 def relayout(basis, xe, wide):
@@ -164,14 +162,18 @@
         lax.fori_loop(0, 8, body, 0)
 
 
-def gram(xe, rows, count):
-    def body(k, acc):
-        x, y = k // 8, k % 8
-        left = xe[x + 1, y + 1, rows, :]
-        right = xe[x + 1, y + 1]
-        return acc + lax.dot_general(left, right, NT, preferred_element_type=F32)
-
-    return lax.fori_loop(0, 16, body, jnp.zeros((count, 256), F32))
+def own_planes(xe, rows):
+    return jnp.concatenate([xe[1 + x, 1 + y, rows, :] for x in range(2) for y in range(8)], axis=1)
+
+
+def gram(left, right):
+    return lax.dot_general(left, right, NT, preferred_element_type=F32)
+
+
+def pack(src, k, v):
+    size = src.shape[1]
+    for i in range(v.shape[0] // size):
+        src[k + i] = v[i * size : (i + 1) * size]
 
 
 def project(f_full, g):
@@ -185,28 +187,71 @@
     both = first_b + second_b
     pad = jnp.zeros((C, 256), F32)
     lane = lax.broadcasted_iota(jnp.int32, (C, 128), 1)
-    row = lax.broadcasted_iota(jnp.int32, (C, 128), 0)
     own = pltpu.roll(f_full[:, 128:256], 64, 1)
     square = (
         own
         - fdot(first, jnp.concatenate([both, pad], axis=0), NT)
         - fdot(both, jnp.concatenate([rest, pad], axis=0), NT)
     )
-    system = jnp.where(lane < C, square, jnp.where(lane == row + C, 1.0, 0.0))
+    system = jnp.where(lane < C, square, 0.0)
     return first + second, both, rest, system
 
 
-def factor(m):
+def splat(v, lane):
+    return jnp.broadcast_to(v[:, lane:lane + 1], (8, 128))
+
+
+def eliminate(m):
+    sub = lax.broadcasted_iota(jnp.int32, (8, 128), 0)
+    out = [None] * 8
+    for j in range(0, 64, 4):
+        t, q = j // 8, j % 8
+        r = [jnp.broadcast_to(m[t][q + a : q + a + 1, :], (8, 128)) for a in range(4)]
+        p = [[splat(r[a], j + b) if b >= a else None for b in range(4)] for a in range(4)]
+        det = p[0][0] * p[1][1] - p[0][1] * p[0][1]
+        inv = 1.0 / det
+        y = [[(p[1][1] * p[0][b] - p[0][1] * p[1][b]) * inv, (p[0][0] * p[1][b] - p[0][1] * p[0][b]) * inv] for b in (2, 3)]
+        s22 = p[2][2] - p[0][2] * y[0][0] - p[1][2] * y[0][1]
+        s23 = p[2][3] - p[0][2] * y[1][0] - p[1][2] * y[1][1]
+        s33 = p[3][3] - p[0][3] * y[1][0] - p[1][3] * y[1][1]
+        det2 = s22 * s33 - s23 * s23
+        r2 = r[2] - y[0][0] * r[0] - y[0][1] * r[1]
+        r3 = r[3] - y[1][0] * r[0] - y[1][1] * r[1]
+        if j < 60:
+            inv2 = 1.0 / det2
+            x0 = (p[1][1] * r[0] - p[0][1] * r[1]) * inv
+            x1 = (p[0][0] * r[1] - p[0][1] * r[0]) * inv
+            x2 = (s33 * r2 - s23 * r3) * inv2
+            x3 = (s22 * r3 - s23 * r2) * inv2
+            x0 = x0 - y[0][0] * x2 - y[1][0] * x3
+            x1 = x1 - y[0][1] * x2 - y[1][1] * x3
+            for v in range(t if q == 0 else t + 1, 8):
+                c = [splat(m[v], j + b) for b in range(4)]
+                new = m[v] - (c[0] * x0 + c[1] * x1) - (c[2] * x2 + c[3] * x3)
+                m[v] = jnp.where(sub >= 4, new, m[v]) if v == t else new
+        a0 = lax.rsqrt(p[0][0])
+        a1 = lax.rsqrt(det * (1.0 / p[0][0]))
+        a2 = lax.rsqrt(s22)
+        a3 = lax.rsqrt(det2 * (1.0 / s22))
+        u = [r[0] * a0, (r[1] - (p[0][1] * (1.0 / p[0][0])) * r[0]) * a1, r2 * a2, (r3 - (s23 * (1.0 / s22)) * r2) * a3]
+        o = out[t] if q else u[3]
+        for a in range(4):
+            o = jnp.where(sub == q + a, u[a], o)
+        out[t] = o
+    return out
+
+
+def factor(system):
     row = lax.broadcasted_iota(jnp.int32, (C, 128), 0)
-    diag = jnp.ones((C, 128), F32)
-    for j in range(C):
-        top = m[j : j + 1, :]
-        pivot = m[j : j + 1, j : j + 1]
-        diag = jnp.where(row == j, pivot, diag)
-        if j < C - 1:
-            ratio = jnp.where(row > j, m[:, j : j + 1] / pivot, 0.0)
-            m = m - ratio * top
-    return m * lax.rsqrt(diag)
+    lane = lax.broadcasted_iota(jnp.int32, (C, 128), 1)
+    diag = jnp.where(lane == row, system, 0.0)
+    across = jnp.sum(diag, axis=1, keepdims=True)
+    along = jnp.sum(diag, axis=0, keepdims=True)
+    scale = lax.rsqrt(across)
+    unit = lax.rsqrt(along)
+    m = jnp.where(lane < C, system * scale * unit, jnp.where(lane == row + C, scale, 0.0))
+    m = jnp.concatenate(eliminate([m[8 * v : 8 * v + 8] for v in range(8)]), axis=0)
+    return jnp.where(lane < C, m * (along * unit), m)
 
 
 def split(v):
@@ -214,113 +259,134 @@
     return high, (v - high.astype(F32)).astype(BF16)
 
 
+def mixed(weights, v):
+    w = lax.dot_general(jnp.concatenate(weights, axis=0), v, NN, preferred_element_type=F32)
+    return (w[0:C] + w[C : 2 * C]).astype(BF16)
+
+
 def kernel(
     table, basis, cell_map,
     out_block, out_proj, out_tri,
-    xe, wide, coef, src1, parts1, tower1, sum1, src2, parts2, tower2, sum2, gm, halo_sems, sum_sems,
+    xe, wide, coef, gm,
+    src0, parts0, tower0, sum0, src1, parts1, tower1, sum1, src2, parts2, tower2, sum2,
+    halo_sems, sum_sems,
 ):
     place = places()
     s, ycol, z, p, plane, chunk, column, near = place
     barrier = pltpu.get_barrier_semaphore()
     for dev in plane + column + near:
         pl.semaphore_signal(barrier, inc=1, device_id=dev, device_id_type=MESH)
+    zero = Sum(src0, parts0, tower0, sum0, sum_sems.at[0], place)
+    one = Sum(src1, parts1, tower1, sum1, sum_sems.at[1], place)
+    two = Sum(src2, parts2, tower2, sum2, sum_sems.at[2], place)
 
     relayout(basis, xe, wide)
     coefficients(cell_map, table, coef, s, ycol)
+    v = own_planes(xe, pl.ds(0, 192))
+    g = gram(v, v[0:128])
+    pack(src0, 0, g)
+    g = gram(v[128:192], v[128:192])
+    pack(src0, 24, jnp.concatenate([g, g], axis=1))
 
     pl.semaphore_wait(barrier, len(plane + column + near))
     for copy in halo_copies(xe, B2, halo_sems.at[0], near):
         copy.start()
-    for k, rows in ((1, B0), (2, B1)):
-        for copy in halo_copies(xe, rows, halo_sems.at[k], near):
-            copy.start()
+    zero.scatter()
     moved = xe.at[pl.ds(0, 3), pl.ds(0, 8), B2]
     wait_bytes(moved, halo_sems.at[0, 1])
     stencil(xe, B2, IM, coef)
 
-    one = Sum(16, src1, parts1, tower1, sum1, sum_sems.at[0], place)
-    two = Sum(8, src2, parts2, tower2, sum2, sum_sems.at[1], place)
-    g = gram(xe, pl.ds(0, 256), 256)
-    src1[0:256, :] = g[:, 0:128]
-    src1[256:512, :] = g[:, 128:256]
+    x = own_planes(xe, pl.ds(0, 256))
+    f = gram(x[192:256], x)
+    pack(src1, 0, f[:, 0:128])
+    pack(src1, 16, f[:, 128:256])
     one.scatter()
-    for copy in halo_copies(xe, IM, halo_sems.at[3], near):
-        copy.start()
+    zero.climb()
+    for k, rows in ((1, B0), (2, B1), (3, IM)):
+        for copy in halo_copies(xe, rows, halo_sems.at[k], near):
+            copy.start()
     one.climb()
+    zero.spread()
     one.spread()
+    zero.collect()
     one.collect()
 
     scale = 1.0 / (256 * 32 * 128)
-    g = jnp.concatenate([sum1[0:256, :], sum1[256:512, :]], axis=1) * scale
-    gm[...] = g
-    proj, both, rest, system = project(g[192:256, :], g)
+    gm[0:192, 0:128] = sum0[0:24].reshape(192, 128) * scale
+    gm[0:128, 128:192] = jnp.transpose(gm[128:192, 0:128])
+    gm[0:192, 192:256] = jnp.zeros((192, 64), F32)
+    gm[192:256, :] = jnp.zeros((64, 256), F32)
+    gm[128:192, 128:192] = sum0[24:32].reshape(64, 128)[:, 0:64] * scale
+    f = jnp.concatenate([sum1[0:16].reshape(64, 128), sum1[16:32].reshape(64, 128)], axis=1) * scale
+    proj, both, rest, system = project(f, gm[...])
     out_proj[0] = proj
 
     col = lax.broadcasted_iota(jnp.int32, (C, 256), 1)
     row = lax.broadcasted_iota(jnp.int32, (C, 256), 0)
-    high, low = split(jnp.where(col == row + 192, 1.0, -both))
+    weights = split(jnp.where(col == row + 192, 1.0, -both))
     for k in range(4):
         wait_bytes(moved, halo_sems.at[k, 0])
         if k:
             wait_bytes(moved, halo_sems.at[k, 1])
 
-    def correct(k, carry):
-        x, y = k // 10, k % 10
-        v = xe[x, y]
-        w = lax.dot_general(high, v, NN, preferred_element_type=F32)
-        w = w + lax.dot_general(low, v, NN, preferred_element_type=F32)
-        xe[x, y, B0, :] = w.astype(BF16)
+    def correct(x, carry):
+        v = jnp.concatenate([xe[x, y] for y in range(10)], axis=1)
+        w = mixed(weights, v)
+        for y in range(10):
+            xe[x, y, B0, :] = w[:, y * 128 : (y + 1) * 128]
         return carry
 
-    lax.fori_loop(0, 40, correct, 0)
+    lax.fori_loop(0, 4, correct, 0)
     stencil(xe, B0, IM, coef)
 
-    h = gram(xe, pl.ds(128, 128), 128)
-    src2[0:128, :] = h[:, 0:128]
-    src2[128:256, :] = h[:, 128:256]
+    x = own_planes(xe, pl.ds(0, 256))
+    h = gram(x[192:256], x)
+    pack(src2, 0, h[:, 0:128])
+    pack(src2, 16, h[:, 128:256])
     two.scatter()
     two.climb()
 
     done = factor(system)
     out_tri[0] = done
     inverse = pltpu.roll(done, 64, 1)[:, 0:C].astype(BF16).astype(F32)
-    zero = jnp.zeros((C, C), F32)
+    none = jnp.zeros((C, C), F32)
     q_left = fdot(inverse, rest[:, 0:128], NN)
     q_own = fdot(fdot(inverse, system[:, 0:C], NN), inverse, NT)
     gm[128:192, 0:128] = q_left
     gm[0:128, 128:192] = jnp.transpose(q_left)
     gm[128:192, 128:192] = q_own
     twice = jnp.concatenate(
-        [jnp.concatenate([inverse, zero], axis=1), jnp.concatenate([zero, inverse], axis=1)], axis=0
+        [jnp.concatenate([inverse, none], axis=1), jnp.concatenate([none, inverse], axis=1)], axis=0
     )
 
     two.spread()
     two.collect()
-    h = jnp.concatenate([sum2[64:128, :], sum2[192:256, :]], axis=1) * scale
+    h = jnp.concatenate([sum2[0:16].reshape(64, 128), sum2[16:32].reshape(64, 128)], axis=1) * scale
     h = fdot(inverse, h, NN)
-    f_full = jnp.concatenate([h[:, 0:128], fdot(h[:, 128:256], twice, NT)], axis=1)
-    proj, both, rest, system = project(f_full, gm[...])
+    f = jnp.concatenate([h[:, 0:128], fdot(h[:, 128:256], twice, NT)], axis=1)
+    proj, both, rest, system = project(f, gm[...])
     out_proj[1] = proj
     lane = lax.broadcasted_iota(jnp.int32, (C, 128), 1)
-    mixed = jnp.where(lane < C, -both[:, 128:256], jnp.where(lane == lax.broadcasted_iota(jnp.int32, (C, 128), 0) + C, 1.0, 0.0))
-    mixed = fdot(mixed, twice, NN)
-    high2, low2 = split(jnp.concatenate([-both[:, 0:128], mixed], axis=1))
+    unit = lax.broadcasted_iota(jnp.int32, (C, 128), 0) + C
+    right = fdot(jnp.where(lane < C, -both[:, 128:256], jnp.where(lane == unit, 1.0, 0.0)), twice, NN)
+    weights = split(jnp.concatenate([-both[:, 0:128], right], axis=1))
+    w = mixed(weights, own_planes(xe, pl.ds(0, 256)))
     done = factor(system)
     out_tri[1] = done
-    inverse2 = pltpu.roll(done, 64, 1)[:, 0:C].astype(BF16)
+    inverse = pltpu.roll(done, 64, 1)[:, 0:C].astype(BF16)
+    q = lax.dot_general(inverse, w, NN, preferred_element_type=F32)
     for x in range(2):
-
-        def finish(y, carry):
-            v = xe[x + 1, y + 1]
-            w = lax.dot_general(high2, v, NN, preferred_element_type=F32)
-            w = w + lax.dot_general(low2, v, NN, preferred_element_type=F32)
-            wide[pl.ds(y, C, stride=8), :] = lax.dot_general(inverse2, w.astype(BF16), NN, preferred_element_type=F32)
-            return carry
-
-        lax.fori_loop(0, 8, finish, 0)
+        for y in range(8):
+            k = (x * 8 + y) * 128
+            wide[pl.ds(y, C, stride=8), :] = q[:, k : k + 128]
         out_block[:, x] = wide[...].reshape(C, 8, 128).astype(BF16)
+    zero.drain()
     one.drain()
     two.drain()
+
+
+def sum_scratch(size):
+    return [pltpu.VMEM((count, size, 128), F32) for count in (32, 31, 16, 32)]
 
 
 def shards(basis, cell_map, table):
@@ -338,17 +404,12 @@
             pltpu.VMEM((4, 10, 256, 128), BF16),
             pltpu.VMEM((C * 8, 128), F32),
             pltpu.VMEM((16 * 32, 128), F32),
-            pltpu.VMEM((512, 128), F32),
-            pltpu.VMEM((31, 16, 128), F32),
-            pltpu.VMEM((16, 16, 128), F32),
-            pltpu.VMEM((512, 128), F32),
-            pltpu.VMEM((256, 128), F32),
-            pltpu.VMEM((31, 8, 128), F32),
-            pltpu.VMEM((16, 8, 128), F32),
-            pltpu.VMEM((256, 128), F32),
             pltpu.VMEM((256, 256), F32),
+            *sum_scratch(8),
+            *sum_scratch(4),
+            *sum_scratch(4),
             pltpu.SemaphoreType.DMA((4, 2)),
-            pltpu.SemaphoreType.DMA((2, 6)),
+            pltpu.SemaphoreType.DMA((3, 6)),
         ],
         compiler_params=pltpu.CompilerParams(
             collective_id=0, has_side_effects=True, vmem_limit_bytes=40 * 1024 * 1024

time: 105 us -> 78.9 us (0.75)
  Pallas kernels: 99.7 us -> 73.2 us
    pallas_call x1, Pallas kernels: 99.7 us -> 73.2 us  [shards(): pl.pallas_call(kernel, out_shape=(jax.ShapeDtypeStruct((C, 2, 8, 128), BF...]
where the time goes in v2:
time: 78.9 us; the launch traced here: 78.6 us
  Pallas kernels  73.2 us (93%)
  local copies, waits for them, and re-layouts  3.94 us (5%)
    pallas_call x1, Pallas kernels, shards(): pl.pallas_call(kernel, out_shape=(jax.ShapeDtypeStruct((C, 2, 8, 128), BF...  73.2 us
    unnamed x8, local copies, waits for them, and re-layouts  3.92 us

profile of v2, /device:TPU:1, one launch (start us, length us, event | category | flops | bytes accessed | tf_op | source)
XLA Modules:
  0.0 78.6 jit_solution(3759579805701690272)
XLA Ops:
  0.6 0.0 copy-start
  0.6 1.1 %copy-done = bf16[3,64,2,8,128]{4,3,2,1,0:T(8,128)(2,1)S(1)} copy-done((bf16[3,64,2,8,128]{4,3,2,1,0:T(8,128)(2,1)S(1)}, bf16[3,64,2,8,128]{4,3,2,1,0:T(8,128)(2,1)}, u32[]{:S(2)}) %copy-start) | copy-done | bytes 786456
  1.8 0.0 copy-start.1
  1.8 0.7 copy-done.1
  2.5 0.0 copy-start.2
  2.5 0.7 copy-done.2
  3.1 73.2 %shard_map.58 = (bf16[64,2,8,128]{3,2,1,0:T(8,128)(2,1)S(1)}, f32[2,64,256]{2,1,0:T(8,128)S(1)}, f32[2,64,128]{2,1,0:T(8,128)S(1)}) custom-call(f32[8,27]{1,0:T(8,128)S(1)} %copy-done.2, bf16[3,64,2,8,128]{4,3,2,1,0:T(8,128)(2,1)S(1)} %copy-done, s32[2,8,128]{2,1,0:T(8,128)S(1)} %copy-done.1), custom_call_target="tpu_custom_call" | custom-call | tf_op jit(solution)/shard_map/pallas_call | solution.py:394
  76.4 0.1 maximum_bitcast_fusion
  76.5 0.7 pad_maximum_fusion
  77.2 0.7 copy.6
  77.9 0.7 copy.8
  (5 shorter events, 0.0 us)
Async XLA Ops:
  0.6 1.1 %copy-start = (bf16[3,64,2,8,128]{4,3,2,1,0:T(8,128)(2,1)S(1)}, bf16[3,64,2,8,128]{4,3,2,1,0:T(8,128)(2,1)}, u32[]{:S(2)}) copy-start(bf16[3,64,2,8,128]{4,3,2,1,0:T(8,128)(2,1)} %basis.1) | copy-start | bytes 2359300
  1.8 0.7 copy-start.1
  2.5 0.7 copy-start.2

commit v3 on v2

--- a/solution.py
+++ b/solution.py
@@ -143,23 +143,32 @@
             coef[pl.ds(x * 8 * 32 + o, 8, stride=32), :] = c
 
 
-def stencil(xe, rows_in, rows_out, coef):
+def is_own(x, y):
+    return x in (1, 2) and 1 <= y <= 8
+
+
+def stencil(xe, rows_in, rows_out, coef, held=None, local=None):
     for x in range(2):
-
-        def body(y, carry):
-            table = coef.at[pl.ds(pl.multiple_of((x * 8 + y) * 32, 32), 32)]
-            acc = [jnp.zeros((C, 128), F32) for _ in range(3)]
+        for y in range(8):
+            table = coef.at[pl.ds((x * 8 + y) * 32, 32)]
+            acc = [None, None, None]
+            if local is False:
+                acc = [held[x * 8 + y, dz] for dz in range(3)]
             for dx in range(3):
                 for dy in range(3):
+                    if local is not None and is_own(x + dx, y + dy) != local:
+                        continue
                     piece = xe[x + dx, y + dy, rows_in, :].astype(F32)
                     for dz in range(3):
                         o = 9 * dx + 3 * dy + dz
-                        acc[dz] = acc[dz] + table[o : o + 1, :] * piece
-            total = acc[1] + pltpu.roll(acc[0], 1, 1) + pltpu.roll(acc[2], 127, 1)
-            xe[x + 1, y + 1, rows_out, :] = total.astype(BF16)
-            return carry
-
-        lax.fori_loop(0, 8, body, 0)
+                        term = table[o : o + 1, :] * piece
+                        acc[dz] = term if acc[dz] is None else acc[dz] + term
+            if local:
+                for dz in range(3):
+                    held[x * 8 + y, dz] = acc[dz]
+            else:
+                total = acc[1] + pltpu.roll(acc[0], 1, 1) + pltpu.roll(acc[2], 127, 1)
+                xe[x + 1, y + 1, rows_out, :] = total.astype(BF16)
 
 
 def own_planes(xe, rows):
@@ -265,22 +274,32 @@
 
 
 def kernel(
-    table, basis, cell_map,
-    out_block, out_proj, out_tri,
-    xe, wide, coef, gm,
+    table_hbm, basis_hbm, map_hbm,
+    w_hbm, proj_hbm, tri_hbm,
+    out_w, out_proj, out_tri, table, basis, cell_map, xe, wide, coef, held, gm,
     src0, parts0, tower0, sum0, src1, parts1, tower1, sum1, src2, parts2, tower2, sum2,
-    halo_sems, sum_sems,
+    halo_sems, sum_sems, in_sems, out_sems,
 ):
     place = places()
     s, ycol, z, p, plane, chunk, column, near = place
     barrier = pltpu.get_barrier_semaphore()
     for dev in plane + column + near:
         pl.semaphore_signal(barrier, inc=1, device_id=dev, device_id_type=MESH)
+    loads = [
+        pltpu.make_async_copy(basis_hbm, basis, in_sems.at[0]),
+        pltpu.make_async_copy(map_hbm, cell_map, in_sems.at[1]),
+        pltpu.make_async_copy(table_hbm, table, in_sems.at[2]),
+    ]
+    for load in loads:
+        load.start()
     zero = Sum(src0, parts0, tower0, sum0, sum_sems.at[0], place)
     one = Sum(src1, parts1, tower1, sum1, sum_sems.at[1], place)
     two = Sum(src2, parts2, tower2, sum2, sum_sems.at[2], place)
 
+    loads[0].wait()
     relayout(basis, xe, wide)
+    loads[1].wait()
+    loads[2].wait()
     coefficients(cell_map, table, coef, s, ycol)
     v = own_planes(xe, pl.ds(0, 192))
     g = gram(v, v[0:128])
@@ -288,13 +307,14 @@
     g = gram(v[128:192], v[128:192])
     pack(src0, 24, jnp.concatenate([g, g], axis=1))
 
+    stencil(xe, B2, IM, coef, held, True)
     pl.semaphore_wait(barrier, len(plane + column + near))
     for copy in halo_copies(xe, B2, halo_sems.at[0], near):
         copy.start()
     zero.scatter()
     moved = xe.at[pl.ds(0, 3), pl.ds(0, 8), B2]
     wait_bytes(moved, halo_sems.at[0, 1])
-    stencil(xe, B2, IM, coef)
+    stencil(xe, B2, IM, coef, held, False)
 
     x = own_planes(xe, pl.ds(0, 256))
     f = gram(x[192:256], x)
@@ -370,19 +390,47 @@
     unit = lax.broadcasted_iota(jnp.int32, (C, 128), 0) + C
     right = fdot(jnp.where(lane < C, -both[:, 128:256], jnp.where(lane == unit, 1.0, 0.0)), twice, NN)
     weights = split(jnp.concatenate([-both[:, 0:128], right], axis=1))
-    w = mixed(weights, own_planes(xe, pl.ds(0, 256)))
-    done = factor(system)
-    out_tri[1] = done
-    inverse = pltpu.roll(done, 64, 1)[:, 0:C].astype(BF16)
-    q = lax.dot_general(inverse, w, NN, preferred_element_type=F32)
+    out_w[...] = mixed(weights, own_planes(xe, pl.ds(0, 256)))
+    stores = [
+        pltpu.make_async_copy(out_proj, proj_hbm, out_sems.at[0]),
+        pltpu.make_async_copy(out_w, w_hbm, out_sems.at[1]),
+        pltpu.make_async_copy(out_tri, tri_hbm, out_sems.at[2]),
+    ]
+    stores[0].start()
+    stores[1].start()
+    out_tri[1] = factor(system)
+    stores[2].start()
+    zero.drain()
+    one.drain()
+    two.drain()
+    for store in stores:
+        store.wait()
+
+
+def finish(w_hbm, proj_hbm, tri_hbm, out_block, out_proj, out_tri, w, proj, tri, wide, sems):
+    loads = [
+        pltpu.make_async_copy(tri_hbm, tri, sems.at[0]),
+        pltpu.make_async_copy(w_hbm, w, sems.at[1]),
+        pltpu.make_async_copy(proj_hbm, proj, sems.at[2]),
+    ]
+    for load in loads:
+        load.start()
+    for load in loads:
+        load.wait()
+    inverse = pltpu.roll(tri[1], 64, 1)[:, 0:C].astype(BF16)
+    q = lax.dot_general(inverse, w[...], NN, preferred_element_type=F32)
     for x in range(2):
         for y in range(8):
             k = (x * 8 + y) * 128
             wide[pl.ds(y, C, stride=8), :] = q[:, k : k + 128]
         out_block[:, x] = wide[...].reshape(C, 8, 128).astype(BF16)
-    zero.drain()
-    one.drain()
-    two.drain()
+    row = lax.broadcasted_iota(jnp.int32, (C, C), 0)
+    col = lax.broadcasted_iota(jnp.int32, (C, C), 1)
+    first = proj[0]
+    out_proj[0] = jnp.concatenate([first[:, 128:192], first[:, 0:128]], axis=1)
+    out_proj[1] = proj[1][:, 0:192]
+    for step in range(2):
+        out_tri[step] = jnp.where(row >= col, jnp.transpose(tri[step])[0:C], 0.0)
 
 
 def sum_scratch(size):
@@ -391,34 +439,59 @@
 
 def shards(basis, cell_map, table):
     vmem = pl.BlockSpec(memory_space=pltpu.VMEM)
-    block, proj, tri = pl.pallas_call(
+    hbm = pl.BlockSpec(memory_space=pltpu.MemorySpace.HBM)
+    found = pl.pallas_call(
         kernel,
         out_shape=(
-            jax.ShapeDtypeStruct((C, 2, 8, 128), BF16),
+            jax.ShapeDtypeStruct((C, 2048), BF16),
             jax.ShapeDtypeStruct((2, C, 256), F32),
             jax.ShapeDtypeStruct((2, C, 128), F32),
         ),
-        in_specs=[pl.BlockSpec(memory_space=pltpu.SMEM), vmem, vmem],
-        out_specs=(vmem, vmem, vmem),
+        in_specs=[hbm, hbm, hbm],
+        out_specs=(hbm, hbm, hbm),
         scratch_shapes=[
+            pltpu.VMEM((C, 2048), BF16),
+            pltpu.VMEM((2, C, 256), F32),
+            pltpu.VMEM((2, C, 128), F32),
+            pltpu.SMEM((8, 27), F32),
+            pltpu.VMEM((3, C, 2, 8, 128), BF16),
+            pltpu.VMEM((2, 8, 128), jnp.int32),
             pltpu.VMEM((4, 10, 256, 128), BF16),
             pltpu.VMEM((C * 8, 128), F32),
             pltpu.VMEM((16 * 32, 128), F32),
+            pltpu.VMEM((16, 3, C, 128), F32),
             pltpu.VMEM((256, 256), F32),
             *sum_scratch(8),
             *sum_scratch(4),
             *sum_scratch(4),
             pltpu.SemaphoreType.DMA((4, 2)),
             pltpu.SemaphoreType.DMA((3, 6)),
+            pltpu.SemaphoreType.DMA((3,)),
+            pltpu.SemaphoreType.DMA((3,)),
         ],
         compiler_params=pltpu.CompilerParams(
-            collective_id=0, has_side_effects=True, vmem_limit_bytes=40 * 1024 * 1024
+            collective_id=0, has_side_effects=True, vmem_limit_bytes=63 * 1024 * 1024
         ),
     )(table, basis, cell_map)
-    proj = jnp.swapaxes(proj, 1, 2)
-    first = jnp.concatenate([proj[0, 128:192], proj[0, 0:128]], axis=0)
-    lower = jnp.tril(jnp.swapaxes(tri[:, :, 0:C], 1, 2))
-    return block, jnp.stack([first, proj[1, 0:192]]), lower
+    block, proj, lower = pl.pallas_call(
+        finish,
+        out_shape=(
+            jax.ShapeDtypeStruct((C, 2, 8, 128), BF16),
+            jax.ShapeDtypeStruct((2, C, 192), F32),
+            jax.ShapeDtypeStruct((2, C, C), F32),
+        ),
+        in_specs=[hbm, hbm, hbm],
+        out_specs=(vmem, vmem, vmem),
+        scratch_shapes=[
+            pltpu.VMEM((C, 2048), BF16),
+            pltpu.VMEM((2, C, 256), F32),
+            pltpu.VMEM((2, C, 128), F32),
+            pltpu.VMEM((C * 8, 128), F32),
+            pltpu.SemaphoreType.DMA((3,)),
+        ],
+        compiler_params=pltpu.CompilerParams(vmem_limit_bytes=63 * 1024 * 1024),
+    )(*found)
+    return block, jnp.swapaxes(proj, 1, 2), lower
 
 
 def solution(mesh):

time: 78.9 us -> 72.9 us (0.924)
  local copies, waits for them, and re-layouts: 3.94 us -> 0 us
  Pallas kernels: 73.2 us -> 72.1 us
    unnamed x8 -> x0, local copies, waits for them, and re-layouts: 3.92 us -> none
    pallas_call x1 -> x2, Pallas kernels: 73.2 us -> 72.1 us  [the longest x1 70 us: shards(): pl.pallas_call(kernel, out_shape=(jax.ShapeDtypeStruct((C, 2048), BF16),...]
where the time goes in v3:
time: 72.9 us; the launch traced here: 72.7 us
  Pallas kernels  72.1 us (99%)
    pallas_call x1, Pallas kernels, shards(): pl.pallas_call(kernel, out_shape=(jax.ShapeDtypeStruct((C, 2048), BF16),...  70 us
    pallas_call x1, Pallas kernels, shards(): pl.pallas_call(finish, out_shape=(jax.ShapeDtypeStruct((C, 2, 8, 128), BF...  2.07 us

profile of v3, /device:TPU:1, one launch (start us, length us, event | category | flops | bytes accessed | tf_op | source)
XLA Modules:
  0.0 72.7 jit_solution(5518008498461640030)
XLA Ops:
  0.6 70.0 %shard_map.58 = (bf16[64,2048]{1,0:T(8,128)(2,1)}, f32[2,64,256]{2,1,0:T(8,128)}, f32[2,64,128]{2,1,0:T(8,128)}) custom-call(f32[8,27]{1,0:T(8,128)} %table_hbm.1, bf16[3,64,2,8,128]{4,3,2,1,0:T(8,128)(2,1)} %basis_hbm.1, s32[2,8,128]{2,1,0:T(8,128)} %map_hbm.1), custom_call_target="tpu_custom_call" | custom-call | tf_op jit(solution)/shard_map/pallas_call | solution.py:443
  70.7 2.1 %shard_map.59 = (bf16[64,2,8,128]{3,2,1,0:T(8,128)(2,1)}, f32[2,64,192]{2,1,0:T(8,128)}, f32[2,64,64]{2,1,0:T(8,128)}) custom-call(bf16[64,2048]{1,0:T(8,128)(2,1)} %get-tuple-element.9.w_hbm, f32[2,64,256]{2,1,0:T(8,128)} %get-tuple-element.10.proj_hbm, f32[2,64,128]{2,1,0:T(8,128)} %get-tuple-element.11.tri_hbm), custom_call_target="tpu_custom_call" | custom-call | tf_op jit(solution)/shard_map/pallas_call | solution.py:476

commit v4 on v3

--- a/solution.py
+++ b/solution.py
@@ -278,12 +278,13 @@
     w_hbm, proj_hbm, tri_hbm,
     out_w, out_proj, out_tri, table, basis, cell_map, xe, wide, coef, held, gm,
     src0, parts0, tower0, sum0, src1, parts1, tower1, sum1, src2, parts2, tower2, sum2,
-    halo_sems, sum_sems, in_sems, out_sems,
+    halo_sems, sum_sems, in_sems, out_sems, vouched,
 ):
     place = places()
     s, ycol, z, p, plane, chunk, column, near = place
     barrier = pltpu.get_barrier_semaphore()
-    for dev in plane + column + near:
+    greeted = plane + near + column[0:4] + column[11:15]
+    for dev in greeted:
         pl.semaphore_signal(barrier, inc=1, device_id=dev, device_id_type=MESH)
     loads = [
         pltpu.make_async_copy(basis_hbm, basis, in_sems.at[0]),
@@ -308,10 +309,12 @@
     pack(src0, 24, jnp.concatenate([g, g], axis=1))
 
     stencil(xe, B2, IM, coef, held, True)
-    pl.semaphore_wait(barrier, len(plane + column + near))
+    pl.semaphore_wait(barrier, len(greeted))
     for copy in halo_copies(xe, B2, halo_sems.at[0], near):
         copy.start()
     zero.scatter()
+    for dev in (column[3], column[11]):
+        pl.semaphore_signal(vouched, inc=1, device_id=dev, device_id_type=MESH)
     moved = xe.at[pl.ds(0, 3), pl.ds(0, 8), B2]
     wait_bytes(moved, halo_sems.at[0, 1])
     stencil(xe, B2, IM, coef, held, False)
@@ -321,6 +324,7 @@
     pack(src1, 0, f[:, 0:128])
     pack(src1, 16, f[:, 128:256])
     one.scatter()
+    pl.semaphore_wait(vouched, 2)
     zero.climb()
     for k, rows in ((1, B0), (2, B1), (3, IM)):
         for copy in halo_copies(xe, rows, halo_sems.at[k], near):
@@ -468,6 +472,7 @@
             pltpu.SemaphoreType.DMA((3, 6)),
             pltpu.SemaphoreType.DMA((3,)),
             pltpu.SemaphoreType.DMA((3,)),
+            pltpu.SemaphoreType.REGULAR,
         ],
         compiler_params=pltpu.CompilerParams(
             collective_id=0, has_side_effects=True, vmem_limit_bytes=63 * 1024 * 1024

time: 72.9 us -> 69.6 us (0.955)
  Pallas kernels: 72.1 us -> 68.8 us
    pallas_call x1, Pallas kernels: 70 us -> 66.7 us  [shards(): pl.pallas_call(kernel, out_shape=(jax.ShapeDtypeStruct((C, 2048), BF16),...]
where the time goes in v4:
time: 69.6 us; the launch traced here: 69.4 us
  Pallas kernels  68.8 us (99%)
    pallas_call x1, Pallas kernels, shards(): pl.pallas_call(kernel, out_shape=(jax.ShapeDtypeStruct((C, 2048), BF16),...  66.7 us
    pallas_call x1, Pallas kernels, shards(): pl.pallas_call(finish, out_shape=(jax.ShapeDtypeStruct((C, 2, 8, 128), BF...  2.07 us

profile of v4, /device:TPU:1, one launch (start us, length us, event | category | flops | bytes accessed | tf_op | source)
XLA Modules:
  0.0 69.4 jit_solution(12351823404428413741)
XLA Ops:
  0.6 66.7 %shard_map.58 = (bf16[64,2048]{1,0:T(8,128)(2,1)}, f32[2,64,256]{2,1,0:T(8,128)}, f32[2,64,128]{2,1,0:T(8,128)}) custom-call(f32[8,27]{1,0:T(8,128)} %table_hbm.1, bf16[3,64,2,8,128]{4,3,2,1,0:T(8,128)(2,1)} %basis_hbm.1, s32[2,8,128]{2,1,0:T(8,128)} %map_hbm.1), custom_call_target="tpu_custom_call" | custom-call | tf_op jit(solution)/shard_map/pallas_call | solution.py:447
  67.3 2.1 %shard_map.59 = (bf16[64,2,8,128]{3,2,1,0:T(8,128)(2,1)}, f32[2,64,192]{2,1,0:T(8,128)}, f32[2,64,64]{2,1,0:T(8,128)}) custom-call(bf16[64,2048]{1,0:T(8,128)(2,1)} %get-tuple-element.9.w_hbm, f32[2,64,256]{2,1,0:T(8,128)} %get-tuple-element.10.proj_hbm, f32[2,64,128]{2,1,0:T(8,128)} %get-tuple-element.11.tri_hbm), custom_call_target="tpu_custom_call" | custom-call | tf_op jit(solution)/shard_map/pallas_call | solution.py:481

commit v5 on v4

--- a/solution.py
+++ b/solution.py
@@ -25,12 +25,16 @@
     s = lax.axis_index("slab")
     y = lax.axis_index("col")
     z, r = lax.div(s, 8), lax.rem(s, 8)
-    rs = [r] + [lax.rem(r + d, 8) for d in range(1, 8)]
+    x, core = lax.div(r, 2), lax.rem(r, 2)
+    xs = [x] + [lax.rem(x + d, 4) for d in range(1, 4)]
     ys = [y] + [lax.rem(y + d, 4) for d in range(1, 4)]
     zs = [z] + [lax.rem(z + d, 16) for d in range(1, 16)]
-    plane = [(z * 8 + a, b) for i, a in enumerate(rs) for j, b in enumerate(ys) if i or j]
-    chunk = [a * 4 + b for i, a in enumerate(rs) for j, b in enumerate(ys) if i or j]
-    column = [(a * 8 + r, y) for a in zs[1:]]
+    cores = [core, 1 - core]
+    steps = [(i, j, k) for i in range(4) for j in range(4) for k in range(2) if i or j or k]
+    steps.sort(key=lambda t: -(min(t[0], 4 - t[0]) + min(t[1], 4 - t[1]) + t[2] * 0.3))
+    plane = [(z * 8 + xs[i] * 2 + cores[k], ys[j]) for i, j, k in steps]
+    chunk = [(xs[i] * 2 + cores[k]) * 4 + ys[j] for i, j, k in steps]
+    column = {d: (zs[d] * 8 + r, y) for d in sorted(range(1, 16), key=lambda d: -min(d, 16 - d))}
     sl = [s, lax.rem(s + 1, 128), lax.rem(s + 127, 128)]
     near = [(sl[i], ys[j]) for i in (0, 1, 2) for j in (0, 1, 3) if i or j]
     return s, y, z, r * 4 + y, plane, chunk, column, near
@@ -78,13 +82,13 @@
         for k, dev in enumerate(self.plane):
             self.send(self.src.at[self.chunk[k]], self.parts.at[k], 0, dev)
 
-    def climb(self):
+    def climb(self, change=None):
         wait_bytes(self.parts, self.sems.at[1])
         total = self.src[self.mine]
         for k in range(31):
             total = total + self.parts[k]
-        self.tower[self.z] = total
-        for dev in self.column:
+        self.tower[self.z] = total if change is None else change(total)
+        for dev in self.column.values():
             self.send(self.tower.at[self.z], self.tower.at[self.z], 2, dev)
 
     def spread(self):
@@ -147,18 +151,20 @@
     return x in (1, 2) and 1 <= y <= 8
 
 
-def stencil(xe, rows_in, rows_out, coef, held=None, local=None):
+def total_of(acc):
+    return (acc[1] + pltpu.roll(acc[0], 1, 1) + pltpu.roll(acc[2], 127, 1)).astype(BF16)
+
+
+def split_stencil(xe, rows, coef, held, local, put):
     for x in range(2):
         for y in range(8):
             table = coef.at[pl.ds((x * 8 + y) * 32, 32)]
-            acc = [None, None, None]
-            if local is False:
-                acc = [held[x * 8 + y, dz] for dz in range(3)]
+            acc = [None, None, None] if local else [held[x * 8 + y, dz] for dz in range(3)]
             for dx in range(3):
                 for dy in range(3):
-                    if local is not None and is_own(x + dx, y + dy) != local:
+                    if is_own(x + dx, y + dy) != local:
                         continue
-                    piece = xe[x + dx, y + dy, rows_in, :].astype(F32)
+                    piece = xe[x + dx, y + dy, rows, :].astype(F32)
                     for dz in range(3):
                         o = 9 * dx + 3 * dy + dz
                         term = table[o : o + 1, :] * piece
@@ -167,8 +173,25 @@
                 for dz in range(3):
                     held[x * 8 + y, dz] = acc[dz]
             else:
-                total = acc[1] + pltpu.roll(acc[0], 1, 1) + pltpu.roll(acc[2], 127, 1)
-                xe[x + 1, y + 1, rows_out, :] = total.astype(BF16)
+                put(x, y, total_of(acc))
+
+
+def stencil(xe, rows, coef, put):
+    for x in range(2):
+
+        def body(y, carry):
+            table = coef.at[pl.ds(pl.multiple_of((x * 8 + y) * 32, 32), 32)]
+            acc = [jnp.zeros((C, 128), F32) for _ in range(3)]
+            for dx in range(3):
+                for dy in range(3):
+                    piece = xe[x + dx, y + dy, rows, :].astype(F32)
+                    for dz in range(3):
+                        o = 9 * dx + 3 * dy + dz
+                        acc[dz] = acc[dz] + table[o : o + 1, :] * piece
+            put(x, y, total_of(acc))
+            return carry
+
+        lax.fori_loop(0, 8, body, 0)
 
 
 def own_planes(xe, rows):
@@ -276,14 +299,14 @@
 def kernel(
     table_hbm, basis_hbm, map_hbm,
     w_hbm, proj_hbm, tri_hbm,
-    out_w, out_proj, out_tri, table, basis, cell_map, xe, wide, coef, held, gm,
+    out_w, out_proj, out_tri, table, basis, cell_map, xe, wide, coef, held, image, gm,
     src0, parts0, tower0, sum0, src1, parts1, tower1, sum1, src2, parts2, tower2, sum2,
     halo_sems, sum_sems, in_sems, out_sems, vouched,
 ):
     place = places()
     s, ycol, z, p, plane, chunk, column, near = place
     barrier = pltpu.get_barrier_semaphore()
-    greeted = plane + near + column[0:4] + column[11:15]
+    greeted = [column[d] for d in (4, 12, 3, 13, 2, 14, 1, 15)] + plane + near
     for dev in greeted:
         pl.semaphore_signal(barrier, inc=1, device_id=dev, device_id_type=MESH)
     loads = [
@@ -308,16 +331,30 @@
     g = gram(v[128:192], v[128:192])
     pack(src0, 24, jnp.concatenate([g, g], axis=1))
 
-    stencil(xe, B2, IM, coef, held, True)
+    split_stencil(xe, B2, coef, held, True, None)
     pl.semaphore_wait(barrier, len(greeted))
     for copy in halo_copies(xe, B2, halo_sems.at[0], near):
         copy.start()
     zero.scatter()
-    for dev in (column[3], column[11]):
+    for dev in (column[4], column[12]):
         pl.semaphore_signal(vouched, inc=1, device_id=dev, device_id_type=MESH)
+    for k, rows in ((1, B1), (2, B0)):
+        for copy in halo_copies(xe, rows, halo_sems.at[k], near):
+            copy.start()
     moved = xe.at[pl.ds(0, 3), pl.ds(0, 8), B2]
+
+    def put_w(x, y, v):
+        xe[x + 1, y + 1, IM, :] = v
+        image[x * 8 + y, C : 2 * C, :] = v
+
+    def put_at(k):
+        def put(x, y, v):
+            image[x * 8 + y, k * C : (k + 1) * C, :] = v
+
+        return put
+
     wait_bytes(moved, halo_sems.at[0, 1])
-    stencil(xe, B2, IM, coef, held, False)
+    split_stencil(xe, B2, coef, held, False, put_w)
 
     x = own_planes(xe, pl.ds(0, 256))
     f = gram(x[192:256], x)
@@ -326,12 +363,26 @@
     one.scatter()
     pl.semaphore_wait(vouched, 2)
     zero.climb()
-    for k, rows in ((1, B0), (2, B1), (3, IM)):
-        for copy in halo_copies(xe, rows, halo_sems.at[k], near):
-            copy.start()
+    for copy in halo_copies(xe, IM, halo_sems.at[3], near):
+        copy.start()
+    wait_bytes(moved, halo_sems.at[1, 1])
+    stencil(xe, B1, coef, put_at(0))
     one.climb()
+    wait_bytes(moved, halo_sems.at[2, 1])
+    stencil(xe, B0, coef, put_at(2))
     zero.spread()
+    wait_bytes(moved, halo_sems.at[3, 1])
+    stencil(xe, IM, coef, put_at(3))
+    x = own_planes(xe, pl.ds(0, 256))
+    y = jnp.concatenate([image[k] for k in range(16)], axis=1)
+    for i, left in enumerate((x, y)):
+        g = gram(left, y)
+        for k in range(32):
+            for half in range(2):
+                at = 16 * i + 8 * half
+                src2[k, at : at + 8, :] = g[8 * k : 8 * k + 8, 128 * half : 128 * half + 128]
     one.spread()
+    two.scatter()
     zero.collect()
     one.collect()
 
@@ -347,28 +398,26 @@
 
     col = lax.broadcasted_iota(jnp.int32, (C, 256), 1)
     row = lax.broadcasted_iota(jnp.int32, (C, 256), 0)
-    weights = split(jnp.where(col == row + 192, 1.0, -both))
+    mix = jnp.where(col == row + 192, 1.0, -both)
+    empty = jnp.zeros((C, 256), F32)
+    mix_both = jnp.concatenate(
+        [jnp.concatenate([mix, empty], axis=1), jnp.concatenate([empty, mix], axis=1)], axis=0
+    )
+
+    def contract(total):
+        wide_row = jnp.concatenate([total[8 * k : 8 * k + 8] for k in range(4)], axis=1)
+        return fdot(wide_row, mix_both, NT)
+
+    two.climb(contract)
+
     for k in range(4):
         wait_bytes(moved, halo_sems.at[k, 0])
-        if k:
-            wait_bytes(moved, halo_sems.at[k, 1])
-
-    def correct(x, carry):
-        v = jnp.concatenate([xe[x, y] for y in range(10)], axis=1)
-        w = mixed(weights, v)
-        for y in range(10):
-            xe[x, y, B0, :] = w[:, y * 128 : (y + 1) * 128]
-        return carry
-
-    lax.fori_loop(0, 4, correct, 0)
-    stencil(xe, B0, IM, coef)
-
+    weights = split(mix)
     x = own_planes(xe, pl.ds(0, 256))
-    h = gram(x[192:256], x)
-    pack(src2, 0, h[:, 0:128])
-    pack(src2, 16, h[:, 128:256])
-    two.scatter()
-    two.climb()
+    y = jnp.concatenate([image[k] for k in range(16)], axis=1)
+    for rows, v in ((B0, mixed(weights, x)), (IM, mixed(weights, y))):
+        for k in range(16):
+            xe[1 + k // 8, 1 + k % 8, rows, :] = v[:, 128 * k : 128 * k + 128]
 
     done = factor(system)
     out_tri[0] = done
@@ -385,8 +434,10 @@
 
     two.spread()
     two.collect()
-    h = jnp.concatenate([sum2[0:16].reshape(64, 128), sum2[16:32].reshape(64, 128)], axis=1) * scale
-    h = fdot(inverse, h, NN)
+    h = sum2[...].reshape(256, 128) * scale
+    own = fdot(mix, h, NN)
+    h = jnp.concatenate([h[0:128, 0:C], own[:, 0:C], pltpu.roll(own, 64, 1)[:, 0:C]], axis=0)
+    h = fdot(inverse, h, NT)
     f = jnp.concatenate([h[:, 0:128], fdot(h[:, 128:256], twice, NT)], axis=1)
     proj, both, rest, system = project(f, gm[...])
     out_proj[1] = proj
@@ -437,8 +488,8 @@
         out_tri[step] = jnp.where(row >= col, jnp.transpose(tri[step])[0:C], 0.0)
 
 
-def sum_scratch(size):
-    return [pltpu.VMEM((count, size, 128), F32) for count in (32, 31, 16, 32)]
+def sum_scratch(sent, kept):
+    return [pltpu.VMEM((count, size, 128), F32) for count, size in ((32, sent), (31, sent), (16, kept), (32, kept))]
 
 
 def shards(basis, cell_map, table):
@@ -464,10 +515,11 @@
             pltpu.VMEM((C * 8, 128), F32),
             pltpu.VMEM((16 * 32, 128), F32),
             pltpu.VMEM((16, 3, C, 128), F32),
+            pltpu.VMEM((16, 256, 128), BF16),
             pltpu.VMEM((256, 256), F32),
-            *sum_scratch(8),
-            *sum_scratch(4),
-            *sum_scratch(4),
+            *sum_scratch(8, 8),
+            *sum_scratch(4, 4),
+            *sum_scratch(32, 8),
             pltpu.SemaphoreType.DMA((4, 2)),
             pltpu.SemaphoreType.DMA((3, 6)),
             pltpu.SemaphoreType.DMA((3,)),

time: 69.6 us -> 65.3 us (0.938)
  Pallas kernels: 68.8 us -> 64.5 us
    pallas_call x1, Pallas kernels: 66.7 us -> 62.5 us  [shards(): pl.pallas_call(kernel, out_shape=(jax.ShapeDtypeStruct((C, 2048), BF16),...]
where the time goes in v5:
time: 65.3 us; the launch traced here: 65.2 us
  Pallas kernels  64.5 us (99%)
    pallas_call x1, Pallas kernels, shards(): pl.pallas_call(kernel, out_shape=(jax.ShapeDtypeStruct((C, 2048), BF16),...  62.5 us
    pallas_call x1, Pallas kernels, shards(): pl.pallas_call(finish, out_shape=(jax.ShapeDtypeStruct((C, 2, 8, 128), BF...  2.07 us

profile of v5, /device:TPU:1, one launch (start us, length us, event | category | flops | bytes accessed | tf_op | source)
XLA Modules:
  0.0 65.2 jit_solution(13362488840617104568)
XLA Ops:
  0.6 62.5 %shard_map.58 = (bf16[64,2048]{1,0:T(8,128)(2,1)}, f32[2,64,256]{2,1,0:T(8,128)}, f32[2,64,128]{2,1,0:T(8,128)}) custom-call(f32[8,27]{1,0:T(8,128)} %table_hbm.1, bf16[3,64,2,8,128]{4,3,2,1,0:T(8,128)(2,1)} %basis_hbm.1, s32[2,8,128]{2,1,0:T(8,128)} %map_hbm.1), custom_call_target="tpu_custom_call" | custom-call | tf_op jit(solution)/shard_map/pallas_call | solution.py:498
  63.1 2.1 %shard_map.59 = (bf16[64,2,8,128]{3,2,1,0:T(8,128)(2,1)}, f32[2,64,192]{2,1,0:T(8,128)}, f32[2,64,64]{2,1,0:T(8,128)}) custom-call(bf16[64,2048]{1,0:T(8,128)(2,1)} %get-tuple-element.9.w_hbm, f32[2,64,256]{2,1,0:T(8,128)} %get-tuple-element.10.proj_hbm, f32[2,64,128]{2,1,0:T(8,128)} %get-tuple-element.11.tri_hbm), custom_call_target="tpu_custom_call" | custom-call | tf_op jit(solution)/shard_map/pallas_call | solution.py:533

commit v6 on v5

--- a/solution.py
+++ b/solution.py
@@ -338,9 +338,8 @@
     zero.scatter()
     for dev in (column[4], column[12]):
         pl.semaphore_signal(vouched, inc=1, device_id=dev, device_id_type=MESH)
-    for k, rows in ((1, B1), (2, B0)):
-        for copy in halo_copies(xe, rows, halo_sems.at[k], near):
-            copy.start()
+    for copy in halo_copies(xe, B1, halo_sems.at[1], near):
+        copy.start()
     moved = xe.at[pl.ds(0, 3), pl.ds(0, 8), B2]
 
     def put_w(x, y, v):
@@ -363,8 +362,9 @@
     one.scatter()
     pl.semaphore_wait(vouched, 2)
     zero.climb()
-    for copy in halo_copies(xe, IM, halo_sems.at[3], near):
-        copy.start()
+    for k, rows in ((2, B0), (3, IM)):
+        for copy in halo_copies(xe, rows, halo_sems.at[k], near):
+            copy.start()
     wait_bytes(moved, halo_sems.at[1, 1])
     stencil(xe, B1, coef, put_at(0))
     one.climb()
@@ -384,14 +384,14 @@
     one.spread()
     two.scatter()
     zero.collect()
-    one.collect()
-
     scale = 1.0 / (256 * 32 * 128)
     gm[0:192, 0:128] = sum0[0:24].reshape(192, 128) * scale
     gm[0:128, 128:192] = jnp.transpose(gm[128:192, 0:128])
     gm[0:192, 192:256] = jnp.zeros((192, 64), F32)
     gm[192:256, :] = jnp.zeros((64, 256), F32)
     gm[128:192, 128:192] = sum0[24:32].reshape(64, 128)[:, 0:64] * scale
+    one.collect()
+
     f = jnp.concatenate([sum1[0:16].reshape(64, 128), sum1[16:32].reshape(64, 128)], axis=1) * scale
     proj, both, rest, system = project(f, gm[...])
     out_proj[0] = proj

time: 65.3 us -> 64.5 us (0.988)
  Pallas kernels: 64.5 us -> 63.7 us
    pallas_call x1, Pallas kernels: 62.5 us -> 61.7 us  [shards(): pl.pallas_call(kernel, out_shape=(jax.ShapeDtypeStruct((C, 2048), BF16),...]
where the time goes in v6:
time: 64.5 us; the launch traced here: 64.4 us
  Pallas kernels  63.7 us (99%)
    pallas_call x1, Pallas kernels, shards(): pl.pallas_call(kernel, out_shape=(jax.ShapeDtypeStruct((C, 2048), BF16),...  61.7 us
    pallas_call x1, Pallas kernels, shards(): pl.pallas_call(finish, out_shape=(jax.ShapeDtypeStruct((C, 2, 8, 128), BF...  2.07 us

profile of v6, /device:TPU:1, one launch (start us, length us, event | category | flops | bytes accessed | tf_op | source)
XLA Modules:
  0.0 64.4 jit_solution(16402049560023455894)
XLA Ops:
  0.6 61.7 %shard_map.58 = (bf16[64,2048]{1,0:T(8,128)(2,1)}, f32[2,64,256]{2,1,0:T(8,128)}, f32[2,64,128]{2,1,0:T(8,128)}) custom-call(f32[8,27]{1,0:T(8,128)} %table_hbm.1, bf16[3,64,2,8,128]{4,3,2,1,0:T(8,128)(2,1)} %basis_hbm.1, s32[2,8,128]{2,1,0:T(8,128)} %map_hbm.1), custom_call_target="tpu_custom_call" | custom-call | tf_op jit(solution)/shard_map/pallas_call | solution.py:498
  62.3 2.1 %shard_map.59 = (bf16[64,2,8,128]{3,2,1,0:T(8,128)(2,1)}, f32[2,64,192]{2,1,0:T(8,128)}, f32[2,64,64]{2,1,0:T(8,128)}) custom-call(bf16[64,2048]{1,0:T(8,128)(2,1)} %get-tuple-element.9.w_hbm, f32[2,64,256]{2,1,0:T(8,128)} %get-tuple-element.10.proj_hbm, f32[2,64,128]{2,1,0:T(8,128)} %get-tuple-element.11.tri_hbm), custom_call_target="tpu_custom_call" | custom-call | tf_op jit(solution)/shard_map/pallas_call | solution.py:533
